TPU v7x, 32 devices: a whole 2x2x4 slice. The times are simulated.
32 devices in a mesh: group: 2 (over x), fiber: 16 (over z, y, core).
Axes of the slice: x: 2, y: 2, z: 4, core: 2. Of those that a mesh axis runs over, the one named last changes fastest.
Arguments:
- traces: bfloat16 [1536, 50176], P(('group', 'fiber')), parts along dimension 0, may hold values from -32 to 32
- live_mask: int32 [1536], P(('group', 'fiber')), parts along dimension 0, may hold values from 0 to 1
- source_channels: int32 [4, 8], P('group'), parts along dimension 0, may hold values from 0 to 47
- source_owner: int32 [4], P('group'), parts along dimension 0, may hold values from 0 to 15
Outputs:
- cross_spectra: float32 [2, 8, 1536, 2048], P(None, None, ('group', 'fiber')), parts along dimension 2
There are 2 independent parts, one for each index of `group`. A program takes and returns all parts, laid end to end along the dimension named above; each array names one. Nothing has to cross between parts.
All inputs are finite; a program needn't handle non-finite values.
Results may differ from a plain program's by a relative error of at most 0.00073.
Values may be sent and summed in bfloat16 or wider, within the bound.
A program may use at most 128 MiB of HBM per device.

v0:
```python
import functools

import jax
import jax.numpy as jnp
import numpy as np
from jax import lax
from jax.experimental import pallas as pl
from jax.experimental.pallas import tpu as pltpu
from jax.sharding import PartitionSpec as P

FRAME = 2048
HOP = FRAME // 2
BINS = FRAME // 2
SMOOTH = 64
RIM = 8
LANES = 128
VMEM = 56 * 1024 * 1024


def dft_table():
    n = np.arange(FRAME)
    k = np.arange(BINS)
    phase = 2.0 * np.pi / FRAME * (n[:, None] * k[None, :] % FRAME)
    hann = 0.5 - 0.5 * np.cos(2.0 * np.pi / FRAME * n)
    table = np.concatenate(
        [hann[:, None] * np.cos(phase), -hann[:, None] * np.sin(phase)], axis=1
    )
    return table.astype(np.float32).astype(jnp.bfloat16)


def band_matrix():
    k = np.arange(BINS)
    inside = np.abs(k[:, None] - k[None, :]) <= SMOOTH
    recip = (1.0 / inside.sum(axis=0)).astype(np.float32)
    return inside.astype(np.float32).astype(jnp.bfloat16), recip[None, :]


def tap_matrix(channels):
    place = np.concatenate(
        [np.arange(channels), np.arange(-RIM, 0), np.arange(channels, channels + RIM)]
    )
    distance = np.abs(np.arange(channels)[:, None] - place[None, :])
    taps = np.where(distance <= RIM, -(RIM + 1.0 - distance), 0.0)
    return np.where(distance == 0, RIM * (RIM + 1.0), taps).astype(np.float32)


def filter_kernel(channels, weight_ref, own_ref, low_ref, high_ref, out_ref, src_ref):
    rows = jnp.concatenate([own_ref[...], low_ref[...], high_ref[...]], axis=0)
    total = jnp.dot(weight_ref[...], rows, preferred_element_type=jnp.float32)
    total = (total * (1.0 / (RIM * (RIM + 1.0)))).astype(jnp.bfloat16)
    out_ref[...] = total[:channels]
    src_ref[...] = total[channels:]


def spatial_filter(weight, own, low, high):
    channels, samples = own.shape
    sources = weight.shape[0] - channels
    blocks = samples // HOP
    chunk = HOP * (7 if blocks % 7 == 0 else 1)
    columns = lambda rows: pl.BlockSpec((rows, chunk), lambda i: (0, i))
    return pl.pallas_call(
        functools.partial(filter_kernel, channels),
        grid=(samples // chunk,),
        in_specs=[
            pl.BlockSpec(weight.shape, lambda i: (0, 0)),
            columns(channels),
            columns(RIM),
            columns(RIM),
        ],
        out_specs=[columns(channels), columns(sources)],
        out_shape=[
            jax.ShapeDtypeStruct((channels, samples), jnp.bfloat16),
            jax.ShapeDtypeStruct((sources, samples), jnp.bfloat16),
        ],
        compiler_params=pltpu.CompilerParams(vmem_limit_bytes=VMEM),
        name="spatial_filter",
    )(weight, own, low, high)


def whiten_kernel(count, x_ref, table_ref, band_ref, recip_ref, out_ref, spec_ref, pow_ref):
    rows = x_ref.shape[0]
    first = pl.program_id(0) * count
    frames = jnp.concatenate(
        [
            x_ref[:, pl.ds(pl.multiple_of((first + i) * HOP, HOP), FRAME)]
            for i in range(count)
        ],
        axis=0,
    )
    width = 256
    for lo in range(0, BINS, width):
        real = jnp.dot(
            frames, table_ref[:, lo : lo + width], preferred_element_type=jnp.float32
        )
        imag = jnp.dot(
            frames,
            table_ref[:, BINS + lo : BINS + lo + width],
            preferred_element_type=jnp.float32,
        )
        spec_ref[:, lo : lo + width] = real
        spec_ref[:, BINS + lo : BINS + lo + width] = imag
        pow_ref[:, lo : lo + width] = (real * real + imag * imag).astype(jnp.bfloat16)
    for lo in range(0, BINS, width):
        start, stop = max(0, lo - LANES), min(BINS, lo + width + LANES)
        smooth = jnp.dot(
            pow_ref[:, start:stop],
            band_ref[start:stop, lo : lo + width],
            preferred_element_type=jnp.float32,
        )
        factor = lax.rsqrt(smooth * recip_ref[:, lo : lo + width] + 1e-06)
        for at in (lo, BINS + lo):
            white = (spec_ref[:, at : at + width] * factor).astype(jnp.bfloat16)
            for i in range(count):
                out_ref[i, :, at : at + width] = white[i * rows : (i + 1) * rows]


def whiten(filtered, count):
    rows, samples = filtered.shape
    frames = samples // HOP - 1
    band, recip = band_matrix()
    whole = lambda shape: pl.BlockSpec(
        shape, lambda i: (0,) * len(shape), pipeline_mode=pl.Buffered(1)
    )
    return pl.pallas_call(
        functools.partial(whiten_kernel, count),
        grid=(frames // count,),
        in_specs=[
            whole((rows, samples)),
            whole((FRAME, FRAME)),
            whole((BINS, BINS)),
            whole((1, BINS)),
        ],
        out_specs=pl.BlockSpec((count, rows, FRAME), lambda i: (i, 0, 0)),
        out_shape=jax.ShapeDtypeStruct((frames, rows, FRAME), jnp.bfloat16),
        scratch_shapes=[
            pltpu.VMEM((count * rows, FRAME), jnp.float32),
            pltpu.VMEM((count * rows, BINS), jnp.bfloat16),
        ],
        compiler_params=pltpu.CompilerParams(vmem_limit_bytes=VMEM),
        cost_estimate=pl.CostEstimate(
            flops=2 * frames * rows * FRAME * FRAME,
            bytes_accessed=8 * FRAME * FRAME,
            transcendentals=frames * rows * BINS,
        ),
        name="whiten",
    )(filtered, dft_table(), band, recip)


def cross_kernel(sr_ref, si_ref, wr_ref, wi_ref, out_ref, c_ref, d_ref, e_ref, a_ref, p_ref, m_ref):
    frames, sources, _ = sr_ref.shape
    channels = wr_ref.shape[1]
    at = pl.multiple_of(pl.program_id(0) * LANES, LANES)

    @pl.loop(0, frames)
    def _(f):
        c = wr_ref[f].astype(jnp.float32)
        d = wi_ref[f].astype(jnp.float32)
        c_ref[f] = c
        d_ref[f] = d
        e_ref[f] = c + d
        a = sr_ref[f].astype(jnp.float32) * (1.0 / frames)
        b = si_ref[f].astype(jnp.float32) * (1.0 / frames)
        a_ref[f] = a
        p_ref[f] = a + b
        m_ref[f] = b - a

    pieces = channels // 8
    together = 2
    for s in range(0, sources, together):

        def step(f, sums):
            sums = list(sums)
            taps = []
            for t in range(together):
                row = pl.ds(s + t, 1)
                taps.append(
                    tuple(
                        jnp.broadcast_to(ref[f, row, :], (8, LANES))
                        for ref in (a_ref, p_ref, m_ref)
                    )
                )
            for v in range(pieces):
                part = slice(8 * v, 8 * v + 8)
                c, d, e = c_ref[f, part, :], d_ref[f, part, :], e_ref[f, part, :]
                for t in range(together):
                    a, p, m = taps[t]
                    base = 3 * (t * pieces + v)
                    sums[base] = sums[base] + a * e
                    sums[base + 1] = sums[base + 1] + p * c
                    sums[base + 2] = sums[base + 2] + m * d
            return tuple(sums)

        zero = jnp.zeros((8, LANES), jnp.float32)
        sums = lax.fori_loop(0, frames, step, (zero,) * (3 * together * pieces), unroll=4)
        for t in range(together):
            for v in range(pieces):
                base = 3 * (t * pieces + v)
                part = slice(8 * v, 8 * v + 8)
                out_ref[s + t, part, pl.ds(at, LANES)] = sums[base] + sums[base + 2]
                out_ref[s + t, part, pl.ds(BINS + at, LANES)] = sums[base] - sums[base + 1]


def cross(sources, whitened):
    frames, channels, _ = whitened.shape
    count = sources.shape[1]
    tiles = BINS // LANES
    real = lambda rows: pl.BlockSpec((frames, rows, LANES), lambda j: (0, 0, j))
    imag = lambda rows: pl.BlockSpec((frames, rows, LANES), lambda j: (0, 0, tiles + j))
    tile = lambda rows: pltpu.VMEM((frames, rows, LANES), jnp.float32)
    return pl.pallas_call(
        cross_kernel,
        grid=(tiles,),
        in_specs=[real(count), imag(count), real(channels), imag(channels)],
        out_specs=pl.BlockSpec(
            (count, channels, FRAME), lambda j: (0, 0, 0), pipeline_mode=pl.Buffered(1)
        ),
        out_shape=jax.ShapeDtypeStruct((count, channels, FRAME), jnp.float32),
        scratch_shapes=[tile(channels)] * 3 + [tile(count)] * 3,
        compiler_params=pltpu.CompilerParams(vmem_limit_bytes=VMEM),
        name="cross",
    )(sources, sources, whitened, whitened)


def neighbours(live, traces):
    count = lax.axis_size("fiber")
    up = [(i, i + 1) for i in range(count - 1)]
    down = [(i + 1, i) for i in range(count - 1)]
    mask = live.astype(jnp.bfloat16)[:, None]
    low = lax.ppermute(traces[-RIM:] * mask[-RIM:], "fiber", up)
    high = lax.ppermute(traces[:RIM] * mask[:RIM], "fiber", down)
    return low, high


def filter_weights(live, source_channels, source_owner):
    channels = live.shape[0]
    alive = live.astype(jnp.float32)
    column = jnp.concatenate([alive, jnp.ones((2 * RIM,), jnp.float32)])
    weight = tap_matrix(channels) * alive[:, None] * column[None, :]
    mine = (source_owner == lax.axis_index("fiber"))[:, None]
    chosen = jnp.where(mine, source_channels, -1).reshape(-1)
    pick = chosen[:, None] == jnp.arange(channels)[None, :]
    picked = jnp.sum(jnp.where(pick[:, :, None], weight[None], 0.0), axis=1)
    return jnp.concatenate([weight, picked], axis=0).astype(jnp.bfloat16)


def on_device(traces, live_mask, source_channels, source_owner):
    steps, per_step = source_channels.shape
    low, high = neighbours(live_mask, traces)
    weight = filter_weights(live_mask, source_channels, source_owner)
    filtered, mine = spatial_filter(weight, traces, low, high)
    arrived = lax.psum(mine, "fiber")
    whitened = whiten(filtered, 8)
    sources = whiten(arrived, 16)
    out = cross(sources, whitened)
    return out.reshape(steps, per_step, live_mask.shape[0], FRAME)


def solution(mesh):
    placed = (P(("group", "fiber"), None), P(("group", "fiber")), P("group", None), P("group"))
    return jax.shard_map(
        on_device,
        mesh=mesh,
        in_specs=placed,
        out_specs=P(None, None, ("group", "fiber"), None),
        check_vma=False,
    )
```

profile of v0, /device:TPU:0, one launch (start us, length us, event | category | flops | bytes accessed | tf_op | source)
XLA Modules:
  0.0 206.1 jit_solution(14587000193757264887)
XLA Ops:
  6.5 0.0 all-reduce.3.cloned.1.call-start
  6.5 0.7 fusion.2
  7.3 0.1 fusion.1
  7.3 1.6 slice_multiply_fusion
  8.9 1.3 collective-permute-start.1
  10.2 3.1 %collective-permute-start = (bf16[8,50176]{1,0:T(8,128)(2,1)S(1)}, bf16[8,50176]{1,0:T(8,128)(2,1)S(1)}, u32[]{:S(2)}, u32[]{:S(2)}) collective-permute-start(bf16[8,50176]{1,0:T(8,128)(2,1)S(1)} %get-tuple-element.10), channel_id=1, source_target_pairs={{0,1},{1,2},{2,3},{3,4},{4,5},{5,6},{6,7},{7,8},{8,9},{9,10},{10,1... | collective-permute-start | bytes 2408456 | tf_op jit(solution)/shard_map/ppermute | solution.py:229
  13.3 0.7 broadcast_compare_fusion
  14.0 0.7 broadcast_select_fusion
  14.7 0.1 eq.27
  14.8 0.1 iota_compare_fusion
  14.9 0.8 fusion
  15.7 0.2 select_reduce_fusion
  15.9 0.6 pad_maximum_fusion.weight_ref
  16.5 0.0 collective-permute-done.1.high_ref
  16.5 0.0 copy-start
  16.5 0.0 collective-permute-done.low_ref
  16.5 0.9 copy-done
  17.4 0.9 copy-done.1
  18.3 9.3 %spatial_filter.1 = (bf16[48,50176]{1,0:T(8,128)(2,1)}, bf16[16,50176]{1,0:T(8,128)(2,1)}) custom-call(bf16[64,64]{1,0:T(8,128)(2,1)} %pad_maximum_fusion.weight_ref, bf16[48,50176]{1,0:T(8,128)(2,1)} %own_ref.1, bf16[8,50176]{1,0:T(8,128)(2,1)} %copy-done.1, bf16[8,50176]{1,0:T(8,128)(2,1)} %copy-done), custom_call_target="tpu_custom_call" | custom-call | tf_op jit(solution)/shard_map/spatial_filter/pallas_call | solution.py:61
  27.5 0.0 all-reduce.3.cloned.1.call-update
  27.6 30.7 %whiten.3.wr_ref.wi_ref = bf16[48,48,2048]{2,1,0:T(8,128)(2,1)} custom-call(bf16[48,50176]{1,0:T(8,128)(2,1)} %get-tuple-element.8.x_ref, bf16[2048,2048]{1,0:T(8,128)(2,1)} %constant.19.clone.table_ref, bf16[1024,1024]{1,0:T(8,128)(2,1)} %constant.20.clone.band_ref, f32[1,1024]{1,0:T(1,128)} %constant.21.clone.recip_ref), custom_call_target="tpu_custom_call" | custom-call | flops 19327352832 | bytes 33554432 | tf_op jit(solution)/shard_map/whiten/pallas_call | solution.py:124
  58.3 81.0 %all-reduce.3.cloned.1.call-done.x_ref = bf16[16,50176]{1,0:T(8,128)(2,1)} async-done(((bf16[16,50176]{1,0:T(8,128)(2,1)}), bf16[16,50176]{1,0:T(8,128)(2,1)}) %all-reduce.3.cloned.1.call-update) | async-done | bytes 1605648 | tf_op jit(solution)/shard_map/psum | solution.py:251
  139.3 13.5 %whiten.2.sr_ref.si_ref = bf16[48,16,2048]{2,1,0:T(8,128)(2,1)} custom-call(bf16[16,50176]{1,0:T(8,128)(2,1)} %all-reduce.3.cloned.1.call-done.x_ref, bf16[2048,2048]{1,0:T(8,128)(2,1)} %constant.19.clone.table_ref, bf16[1024,1024]{1,0:T(8,128)(2,1)} %constant.20.clone.band_ref, f32[1,1024]{1,0:T(1,128)} %constant.21.clone.recip_ref), custom_call_target="tpu_custom_call" | custom-call | flops 6442450944 | bytes 33554432 | tf_op jit(solution)/shard_map/whiten/pallas_call | solution.py:124
  152.9 46.4 %cross.1 = f32[16,48,2048]{2,1,0:T(8,128)} custom-call(bf16[48,16,2048]{2,1,0:T(8,128)(2,1)} %whiten.2.sr_ref.si_ref, bf16[48,16,2048]{2,1,0:T(8,128)(2,1)} %whiten.2.sr_ref.si_ref, bf16[48,48,2048]{2,1,0:T(8,128)(2,1)} %whiten.3.wr_ref.wi_ref, bf16[48,48,2048]{2,1,0:T(8,128)(2,1)} %whiten.3.wr_ref.wi_ref), custom_call_target="tpu_custom_call" | custom-call | tf_op jit(solution)/shard_map/cross/pallas_call | solution.py:210
  (2 shorter events, 0.0 us)
Async XLA Ops:
  6.5 132.8 %all-reduce.3.cloned.1.call-start = ((), (), s32[]{:S(2)}) async-start(), calls=%async_computation | async-start | bytes 3211264 | tf_op jit(solution)/shard_map/psum | solution.py:251
  8.9 7.6 %collective-permute-start.1 = (bf16[8,50176]{1,0:T(8,128)(2,1)S(1)}, bf16[8,50176]{1,0:T(8,128)(2,1)S(1)}, u32[]{:S(2)}, u32[]{:S(2)}) collective-permute-start(bf16[8,50176]{1,0:T(8,128)(2,1)S(1)} %get-tuple-element.9), channel_id=1, source_target_pairs={{1,0},{2,1},{3,2},{4,3},{5,4},{6,5},{7,6},{8,7},{9,8},{10,9},{11,1... | collective-permute-start | bytes 2408456 | tf_op jit(solution)/shard_map/ppermute | solution.py:230
  10.2 6.3 %collective-permute-start = (bf16[8,50176]{1,0:T(8,128)(2,1)S(1)}, bf16[8,50176]{1,0:T(8,128)(2,1)S(1)}, u32[]{:S(2)}, u32[]{:S(2)}) collective-permute-start(bf16[8,50176]{1,0:T(8,128)(2,1)S(1)} %get-tuple-element.10), channel_id=1, source_target_pairs={{0,1},{1,2},{2,3},{3,4},{4,5},{5,6},{6,7},{7,8},{8,9},{9,10},{10,1... | collective-permute-start | bytes 2408456 | tf_op jit(solution)/shard_map/ppermute | solution.py:229
  16.5 0.9 copy-start
  17.4 0.9 copy-start.1
Sparse Core Ops, SparseCore 0:
  27.7 111.5 all-reduce.2
where the time goes:
time: 207 us; the launch traced here: 206 us
  Pallas kernels  99.9 us (48%)
  waiting for transfers between devices  81.1 us (39%)
  between operations  13.4 us (6%)
  other arithmetic  5.39 us (3%)
  starting transfers between devices  4.38 us (2%)
    psum x1, waiting for transfers between devices, on_device(): arrived = lax.psum(mine, 'fiber')  81 us
    pallas_call x1, Pallas kernels, cross(): pl.pallas_call(cross_kernel, grid=(tiles,), in_specs=[real(count), imag(c...  46.4 us
    pallas_call x2, Pallas kernels, whiten(): pl.pallas_call(functools.partial(whiten_kernel, count), grid=(frames // c...  44.2 us
    pallas_call x1, Pallas kernels, spatial_filter(): pl.pallas_call(functools.partial(filter_kernel, channels), grid=(samples...  9.25 us
  transfers between devices with their start and end apart: 3, of which 1 were waited for; matrix products, arithmetic and copies ran while one was open for 2% of the time, Pallas kernels for 15%

commit v1 on v0

--- a/solution.py
+++ b/solution.py
@@ -221,6 +221,100 @@
     )(sources, sources, whitened, whitened)
 
 
+def share_stages(size):
+    return [1 << i for i in range(size.bit_length() - 1)]
+
+
+def share_kernel(size, x_ref, out_ref, held, landed, result, send_sem, recv_sem):
+    me = lax.axis_index("fiber")
+    stages = share_stages(size)
+    samples = x_ref.shape[1]
+    length = held.shape[2]
+    sides = [lax.rem(me // bit, 2) for bit in stages]
+    partners = [me + bit - 2 * bit * side for bit, side in zip(stages, sides)]
+
+    barrier = pltpu.get_barrier_semaphore()
+    for partner in partners:
+        pl.semaphore_signal(
+            barrier,
+            inc=1,
+            device_id={"fiber": partner},
+            device_id_type=pl.DeviceIdType.MESH,
+        )
+    for j in range(size):
+        stop = min(samples, (j + 1) * length)
+        if stop < (j + 1) * length:
+            held[j] = jnp.zeros(held.shape[1:], held.dtype)
+        if stop > j * length:
+            held[j, :, : stop - j * length] = x_ref[:, j * length : stop]
+    pl.semaphore_wait(barrier, len(stages))
+
+    first, count, at = 0, size, 0
+    firsts = []
+    for i, side in enumerate(sides):
+        count //= 2
+        firsts.append(first)
+        kept = first + side * count
+        sent = first + (1 - side) * count
+        copy = pltpu.make_async_remote_copy(
+            src_ref=held.at[pl.ds(sent, count)],
+            dst_ref=landed.at[pl.ds(at, count)],
+            send_sem=send_sem.at[i],
+            recv_sem=recv_sem.at[i],
+            device_id={"fiber": partners[i]},
+            device_id_type=pl.DeviceIdType.MESH,
+        )
+        copy.start()
+        copy.wait()
+        for j in range(count):
+            held[kept + j] = held[kept + j] + landed[at + j]
+        at += count
+        first = kept
+    result[first] = held[first]
+    for i in reversed(range(len(stages))):
+        copy = pltpu.make_async_remote_copy(
+            src_ref=result.at[pl.ds(first, count)],
+            dst_ref=result.at[pl.ds(first, count)],
+            send_sem=send_sem.at[len(stages) + i],
+            recv_sem=recv_sem.at[len(stages) + i],
+            device_id={"fiber": partners[i]},
+            device_id_type=pl.DeviceIdType.MESH,
+        )
+        copy.start()
+        copy.wait()
+        first = firsts[i]
+        count *= 2
+    for j in range(size):
+        stop = min(samples, (j + 1) * length)
+        if stop > j * length:
+            out_ref[:, j * length : stop] = result[j, :, : stop - j * length]
+
+
+def share(mine):
+    rows, samples = mine.shape
+    size = lax.axis_size("fiber")
+    length = -(-samples // (size * LANES)) * LANES
+    stages = len(share_stages(size))
+    blocks = lambda count: pltpu.VMEM((count, rows, length), jnp.bfloat16)
+    return pl.pallas_call(
+        functools.partial(share_kernel, size),
+        in_specs=[pl.BlockSpec(memory_space=pltpu.VMEM)],
+        out_specs=pl.BlockSpec(memory_space=pltpu.VMEM),
+        out_shape=jax.ShapeDtypeStruct((rows, samples), jnp.bfloat16),
+        scratch_shapes=[
+            blocks(size),
+            blocks(size),
+            blocks(size),
+            pltpu.SemaphoreType.DMA((2 * stages,)),
+            pltpu.SemaphoreType.DMA((2 * stages,)),
+        ],
+        compiler_params=pltpu.CompilerParams(
+            collective_id=0, has_side_effects=True, vmem_limit_bytes=VMEM
+        ),
+        name="share",
+    )(mine)
+
+
 def neighbours(live, traces):
     count = lax.axis_size("fiber")
     up = [(i, i + 1) for i in range(count - 1)]
@@ -248,7 +342,7 @@
     low, high = neighbours(live_mask, traces)
     weight = filter_weights(live_mask, source_channels, source_owner)
     filtered, mine = spatial_filter(weight, traces, low, high)
-    arrived = lax.psum(mine, "fiber")
+    arrived = share(mine)
     whitened = whiten(filtered, 8)
     sources = whiten(arrived, 16)
     out = cross(sources, whitened)

time: 207 us -> 178 us (0.86)
  waiting for transfers between devices: 81.1 us -> 0.01 us
  Pallas kernels: 99.9 us -> 166 us
  between operations: 13.4 us -> 0.04 us
    psum x1 -> x0, waiting for transfers between devices: 81 us -> none  [on_device(): arrived = lax.psum(mine, 'fiber')]
    pallas_call x0 -> x1, Pallas kernels: none -> 66 us  [share(): pl.pallas_call(functools.partial(share_kernel, size), in_specs=[pl.BlockS...]
  transfers between devices with their start and end apart: 3 -> 2, of which waited for: 1 -> 0; matrix products, arithmetic and copies ran while one was open for 2% -> 2% of each run, Pallas kernels for 15% -> 0%
where the time goes in v1:
time: 178 us
  Pallas kernels  166 us (93%)
  other arithmetic  5.39 us (3%)
  starting transfers between devices  4.37 us (2%)
  local copies, waits for them, and re-layouts  1.94 us (1%)
    pallas_call x1, Pallas kernels, share(): pl.pallas_call(functools.partial(share_kernel, size), in_specs=[pl.BlockS...  66 us
    pallas_call x1, Pallas kernels, cross(): pl.pallas_call(cross_kernel, grid=(tiles,), in_specs=[real(count), imag(c...  46.4 us
    pallas_call x2, Pallas kernels, whiten(): pl.pallas_call(functools.partial(whiten_kernel, count), grid=(frames // c...  44.2 us
    pallas_call x1, Pallas kernels, spatial_filter(): pl.pallas_call(functools.partial(filter_kernel, channels), grid=(samples...  9.2 us
  transfers between devices with their start and end apart: 2, of which 0 were waited for; matrix products, arithmetic and copies ran while one was open for 2% of the time, Pallas kernels for 0%

profile of v1, /device:TPU:0, one launch (start us, length us, event | category | flops | bytes accessed | tf_op | source)
XLA Modules:
  0.0 177.6 jit_solution(3561367256494718268)
XLA Ops:
  0.0 0.7 fusion.2
  0.7 0.1 fusion.1
  0.8 1.6 slice_multiply_fusion
  2.4 1.3 collective-permute-start.1
  3.7 3.1 %collective-permute-start = (bf16[8,50176]{1,0:T(8,128)(2,1)S(1)}, bf16[8,50176]{1,0:T(8,128)(2,1)S(1)}, u32[]{:S(2)}, u32[]{:S(2)}) collective-permute-start(bf16[8,50176]{1,0:T(8,128)(2,1)S(1)} %get-tuple-element.10), channel_id=1, source_target_pairs={{0,1},{1,2},{2,3},{3,4},{4,5},{5,6},{6,7},{7,8},{8,9},{9,10},{10,1... | collective-permute-start | bytes 2408456 | tf_op jit(solution)/shard_map/ppermute | solution.py:323
  6.8 0.7 broadcast_compare_fusion
  7.4 0.7 broadcast_select_fusion
  8.2 0.1 eq.27
  8.3 0.1 iota_compare_fusion
  8.3 0.8 fusion
  9.1 0.2 select_reduce_fusion
  9.3 0.6 pad_maximum_fusion.weight_ref
  10.0 0.0 collective-permute-done.1.high_ref
  10.0 0.0 copy-start
  10.0 0.0 collective-permute-done.low_ref
  10.0 0.9 copy-done
  10.9 0.0 copy-start.1
  10.9 0.9 copy-done.1
  11.7 9.2 %spatial_filter.1 = (bf16[48,50176]{1,0:T(8,128)(2,1)}, bf16[16,50176]{1,0:T(8,128)(2,1)}) custom-call(bf16[64,64]{1,0:T(8,128)(2,1)} %pad_maximum_fusion.weight_ref, bf16[48,50176]{1,0:T(8,128)(2,1)} %own_ref.1, bf16[8,50176]{1,0:T(8,128)(2,1)} %copy-done.1, bf16[8,50176]{1,0:T(8,128)(2,1)} %copy-done), custom_call_target="tpu_custom_call" | custom-call | tf_op jit(solution)/shard_map/spatial_filter/pallas_call | solution.py:61
  20.9 66.0 %share.1.x_ref = bf16[16,50176]{1,0:T(8,128)(2,1)} custom-call(bf16[16,50176]{1,0:T(8,128)(2,1)} %get-tuple-element.7.x_ref), custom_call_target="tpu_custom_call" | custom-call | tf_op jit(solution)/shard_map/share/pallas_call | solution.py:299
  86.9 13.6 %whiten.2.sr_ref.si_ref = bf16[48,16,2048]{2,1,0:T(8,128)(2,1)} custom-call(bf16[16,50176]{1,0:T(8,128)(2,1)} %share.1.x_ref, bf16[2048,2048]{1,0:T(8,128)(2,1)} %constant.19.clone.table_ref, bf16[1024,1024]{1,0:T(8,128)(2,1)} %constant.20.clone.band_ref, f32[1,1024]{1,0:T(1,128)} %constant.21.clone.recip_ref), custom_call_target="tpu_custom_call" | custom-call | flops 6442450944 | bytes 33554432 | tf_op jit(solution)/shard_map/whiten/pallas_call | solution.py:124
  100.5 30.7 %whiten.3.wr_ref.wi_ref = bf16[48,48,2048]{2,1,0:T(8,128)(2,1)} custom-call(bf16[48,50176]{1,0:T(8,128)(2,1)} %get-tuple-element.8.x_ref, bf16[2048,2048]{1,0:T(8,128)(2,1)} %constant.19.clone.table_ref, bf16[1024,1024]{1,0:T(8,128)(2,1)} %constant.20.clone.band_ref, f32[1,1024]{1,0:T(1,128)} %constant.21.clone.recip_ref), custom_call_target="tpu_custom_call" | custom-call | flops 19327352832 | bytes 33554432 | tf_op jit(solution)/shard_map/whiten/pallas_call | solution.py:124
  131.2 46.4 %cross.1 = f32[16,48,2048]{2,1,0:T(8,128)} custom-call(bf16[48,16,2048]{2,1,0:T(8,128)(2,1)} %whiten.2.sr_ref.si_ref, bf16[48,16,2048]{2,1,0:T(8,128)(2,1)} %whiten.2.sr_ref.si_ref, bf16[48,48,2048]{2,1,0:T(8,128)(2,1)} %whiten.3.wr_ref.wi_ref, bf16[48,48,2048]{2,1,0:T(8,128)(2,1)} %whiten.3.wr_ref.wi_ref), custom_call_target="tpu_custom_call" | custom-call | tf_op jit(solution)/shard_map/cross/pallas_call | solution.py:210
  (1 shorter events, 0.0 us)
Async XLA Ops:
  2.4 7.6 %collective-permute-start.1 = (bf16[8,50176]{1,0:T(8,128)(2,1)S(1)}, bf16[8,50176]{1,0:T(8,128)(2,1)S(1)}, u32[]{:S(2)}, u32[]{:S(2)}) collective-permute-start(bf16[8,50176]{1,0:T(8,128)(2,1)S(1)} %get-tuple-element.9), channel_id=1, source_target_pairs={{1,0},{2,1},{3,2},{4,3},{5,4},{6,5},{7,6},{8,7},{9,8},{10,9},{11,1... | collective-permute-start | bytes 2408456 | tf_op jit(solution)/shard_map/ppermute | solution.py:324
  3.7 6.3 %collective-permute-start = (bf16[8,50176]{1,0:T(8,128)(2,1)S(1)}, bf16[8,50176]{1,0:T(8,128)(2,1)S(1)}, u32[]{:S(2)}, u32[]{:S(2)}) collective-permute-start(bf16[8,50176]{1,0:T(8,128)(2,1)S(1)} %get-tuple-element.10), channel_id=1, source_target_pairs={{0,1},{1,2},{2,3},{3,4},{4,5},{5,6},{6,7},{7,8},{8,9},{9,10},{10,1... | collective-permute-start | bytes 2408456 | tf_op jit(solution)/shard_map/ppermute | solution.py:323
  10.0 0.9 copy-start
  10.9 0.9 copy-start.1

commit v2 on v0

--- a/solution.py
+++ b/solution.py
@@ -77,9 +77,9 @@
     )(weight, own, low, high)
 
 
-def whiten_kernel(count, x_ref, table_ref, band_ref, recip_ref, out_ref, spec_ref, pow_ref):
+def whiten_frames(x_ref, first, count, tables, out_ref, spec_ref, pow_ref, between=None):
+    table_ref, band_ref, recip_ref = tables
     rows = x_ref.shape[0]
-    first = pl.program_id(0) * count
     frames = jnp.concatenate(
         [
             x_ref[:, pl.ds(pl.multiple_of((first + i) * HOP, HOP), FRAME)]
@@ -87,8 +87,11 @@
         ],
         axis=0,
     )
+    used = slice(0, count * rows)
     width = 256
     for lo in range(0, BINS, width):
+        if between is not None and lo == BINS // 2:
+            between()
         real = jnp.dot(
             frames, table_ref[:, lo : lo + width], preferred_element_type=jnp.float32
         )
@@ -97,53 +100,214 @@
             table_ref[:, BINS + lo : BINS + lo + width],
             preferred_element_type=jnp.float32,
         )
-        spec_ref[:, lo : lo + width] = real
-        spec_ref[:, BINS + lo : BINS + lo + width] = imag
-        pow_ref[:, lo : lo + width] = (real * real + imag * imag).astype(jnp.bfloat16)
+        spec_ref[used, lo : lo + width] = real
+        spec_ref[used, BINS + lo : BINS + lo + width] = imag
+        pow_ref[used, lo : lo + width] = (real * real + imag * imag).astype(jnp.bfloat16)
     for lo in range(0, BINS, width):
         start, stop = max(0, lo - LANES), min(BINS, lo + width + LANES)
         smooth = jnp.dot(
-            pow_ref[:, start:stop],
+            pow_ref[used, start:stop],
             band_ref[start:stop, lo : lo + width],
             preferred_element_type=jnp.float32,
         )
         factor = lax.rsqrt(smooth * recip_ref[:, lo : lo + width] + 1e-06)
         for at in (lo, BINS + lo):
-            white = (spec_ref[:, at : at + width] * factor).astype(jnp.bfloat16)
+            white = (spec_ref[used, at : at + width] * factor).astype(jnp.bfloat16)
             for i in range(count):
                 out_ref[i, :, at : at + width] = white[i * rows : (i + 1) * rows]
 
 
-def whiten(filtered, count):
+def share_stages(size):
+    return [1 << i for i in range(size.bit_length() - 1)]
+
+
+def share_actions(size, x_ref, arrived, held, landed, result, send_sem, recv_sem):
+    me = lax.axis_index("fiber")
+    stages = share_stages(size)
+    samples = x_ref.shape[1]
+    length = held.shape[2]
+    sides = [lax.rem(me // bit, 2) for bit in stages]
+    partners = [me + bit - 2 * bit * side for bit, side in zip(stages, sides)]
+
+    def remote(i, source, target, phase):
+        return pltpu.make_async_remote_copy(
+            src_ref=source,
+            dst_ref=target,
+            send_sem=send_sem.at[phase],
+            recv_sem=recv_sem.at[phase],
+            device_id={"fiber": partners[i]},
+            device_id_type=pl.DeviceIdType.MESH,
+        )
+
+    first, count, at = 0, size, 0
+    copies, ends, spans = [], [], []
+
+    def adding(kept, count, at):
+        def run():
+            for j in range(count):
+                held[kept + j] = held[kept + j] + landed[at + j]
+
+        return run
+
+    for i, side in enumerate(sides):
+        spans.append(first)
+        count //= 2
+        kept = first + side * count
+        sent = first + (1 - side) * count
+        copies.append(
+            remote(i, held.at[pl.ds(sent, count)], landed.at[pl.ds(at, count)], i)
+        )
+        ends.append(adding(kept, count, at))
+        at += count
+        first = kept
+
+    last = first
+
+    def keep():
+        result[last] = held[last]
+
+    for i in reversed(range(len(stages))):
+        part = result.at[pl.ds(first, count)]
+        copies.append(remote(i, part, part, len(stages) + i))
+        ends.append(None)
+        first = spans[i]
+        count *= 2
+
+    def enter():
+        barrier = pltpu.get_barrier_semaphore()
+        for partner in partners:
+            pl.semaphore_signal(
+                barrier,
+                inc=1,
+                device_id={"fiber": partner},
+                device_id_type=pl.DeviceIdType.MESH,
+            )
+        for j in range(size):
+            stop = min(samples, (j + 1) * length)
+            if stop < (j + 1) * length:
+                held[j] = jnp.zeros(held.shape[1:], held.dtype)
+            if stop > j * length:
+                held[j, :, : stop - j * length] = x_ref[:, j * length : stop]
+        pl.semaphore_wait(barrier, len(stages))
+        copies[0].start()
+
+    def middle(phase):
+        def run():
+            copies[phase - 1].wait()
+            if ends[phase - 1] is not None:
+                ends[phase - 1]()
+            if phase == len(stages):
+                keep()
+            copies[phase].start()
+
+        return run
+
+    def leave():
+        copies[-1].wait()
+        for j in range(size):
+            stop = min(samples, (j + 1) * length)
+            if stop > j * length:
+                arrived[:, j * length : stop] = result[j, :, : stop - j * length]
+
+    return [enter] + [middle(phase) for phase in range(1, len(copies))] + [leave]
+
+
+def whiten_kernel(
+    size, own_count, src_count, own_steps,
+    x_ref, mine_ref, table_ref, band_ref, recip_ref,
+    own_ref, src_ref,
+    spec_ref, pow_ref, arrived, held, landed, result, send_sem, recv_sem,
+):
+    step = pl.program_id(0)
+    tables = (table_ref, band_ref, recip_ref)
+    actions = share_actions(
+        size, mine_ref, arrived, held, landed, result, send_sem, recv_sem
+    )
+    slots = 2 * own_steps
+    moves = len(actions) - 1
+    when = [q * slots // moves for q in range(moves)]
+
+    def progress(half):
+        for q, slot in enumerate(when):
+            if slot % 2 == half:
+                pl.when(step == slot // 2)(actions[q])
+
+    @pl.when(step < own_steps)
+    def _():
+        progress(0)
+        whiten_frames(
+            x_ref, step * own_count, own_count, tables, own_ref, spec_ref, pow_ref,
+            lambda: progress(1),
+        )
+
+    pl.when(step == own_steps)(actions[-1])
+
+    @pl.when(step >= own_steps)
+    def _():
+        whiten_frames(
+            arrived, (step - own_steps) * src_count, src_count, tables, src_ref,
+            spec_ref, pow_ref,
+        )
+
+
+def whiten(filtered, mine, own_count, src_count):
     rows, samples = filtered.shape
+    sources = mine.shape[0]
     frames = samples // HOP - 1
+    size = lax.axis_size("fiber")
+    length = -(-samples // (size * LANES)) * LANES
+    phases = 2 * len(share_stages(size))
+    own_steps, src_steps = frames // own_count, frames // src_count
     band, recip = band_matrix()
     whole = lambda shape: pl.BlockSpec(
         shape, lambda i: (0,) * len(shape), pipeline_mode=pl.Buffered(1)
     )
+    blocks = pltpu.VMEM((size, sources, length), jnp.bfloat16)
+    depth = max(own_count * rows, src_count * sources)
     return pl.pallas_call(
-        functools.partial(whiten_kernel, count),
-        grid=(frames // count,),
+        functools.partial(whiten_kernel, size, own_count, src_count, own_steps),
+        grid=(own_steps + src_steps,),
         in_specs=[
             whole((rows, samples)),
+            whole((sources, samples)),
             whole((FRAME, FRAME)),
             whole((BINS, BINS)),
             whole((1, BINS)),
         ],
-        out_specs=pl.BlockSpec((count, rows, FRAME), lambda i: (i, 0, 0)),
-        out_shape=jax.ShapeDtypeStruct((frames, rows, FRAME), jnp.bfloat16),
+        out_specs=[
+            pl.BlockSpec(
+                (own_count, rows, FRAME),
+                lambda i: (i - (i // own_steps) * (i - own_steps + 1), 0, 0),
+            ),
+            pl.BlockSpec(
+                (src_count, sources, FRAME),
+                lambda i: ((i // own_steps) * (i - own_steps), 0, 0),
+            ),
+        ],
+        out_shape=[
+            jax.ShapeDtypeStruct((frames, rows, FRAME), jnp.bfloat16),
+            jax.ShapeDtypeStruct((frames, sources, FRAME), jnp.bfloat16),
+        ],
         scratch_shapes=[
-            pltpu.VMEM((count * rows, FRAME), jnp.float32),
-            pltpu.VMEM((count * rows, BINS), jnp.bfloat16),
-        ],
-        compiler_params=pltpu.CompilerParams(vmem_limit_bytes=VMEM),
+            pltpu.VMEM((depth, FRAME), jnp.float32),
+            pltpu.VMEM((depth, BINS), jnp.bfloat16),
+            pltpu.VMEM((sources, samples), jnp.bfloat16),
+            blocks,
+            blocks,
+            blocks,
+            pltpu.SemaphoreType.DMA((phases,)),
+            pltpu.SemaphoreType.DMA((phases,)),
+        ],
+        compiler_params=pltpu.CompilerParams(
+            collective_id=0, has_side_effects=True, vmem_limit_bytes=VMEM
+        ),
         cost_estimate=pl.CostEstimate(
-            flops=2 * frames * rows * FRAME * FRAME,
+            flops=2 * frames * (rows + sources) * FRAME * FRAME,
             bytes_accessed=8 * FRAME * FRAME,
-            transcendentals=frames * rows * BINS,
+            transcendentals=frames * (rows + sources) * BINS,
         ),
         name="whiten",
-    )(filtered, dft_table(), band, recip)
+    )(filtered, mine, dft_table(), band, recip)
 
 
 def cross_kernel(sr_ref, si_ref, wr_ref, wi_ref, out_ref, c_ref, d_ref, e_ref, a_ref, p_ref, m_ref):
@@ -248,9 +412,7 @@
     low, high = neighbours(live_mask, traces)
     weight = filter_weights(live_mask, source_channels, source_owner)
     filtered, mine = spatial_filter(weight, traces, low, high)
-    arrived = lax.psum(mine, "fiber")
-    whitened = whiten(filtered, 8)
-    sources = whiten(arrived, 16)
+    whitened, sources = whiten(filtered, mine, 8, 24)
     out = cross(sources, whitened)
     return out.reshape(steps, per_step, live_mask.shape[0], FRAME)
 

time: 207 us -> 150 us (0.72)
  waiting for transfers between devices: 81.1 us -> 0.01 us
  Pallas kernels: 99.9 us -> 137 us
  between operations: 13.4 us -> 0.04 us
    psum x1 -> x0, waiting for transfers between devices: 81 us -> none  [on_device(): arrived = lax.psum(mine, 'fiber')]
    pallas_call x2 -> x1, Pallas kernels: 44.2 us -> 81.6 us  [whiten(): pl.pallas_call(functools.partial(whiten_kernel, size, own_count, src_coun...]
  transfers between devices with their start and end apart: 3 -> 2, of which waited for: 1 -> 0; matrix products, arithmetic and copies ran while one was open for 2% -> 2% of each run, Pallas kernels for 15% -> 0%
where the time goes in v2:
time: 150 us; the launch traced here: 149 us
  Pallas kernels  137 us (91%)
  other arithmetic  5.38 us (4%)
  starting transfers between devices  4.37 us (3%)
  local copies, waits for them, and re-layouts  1.97 us (1%)
    pallas_call x1, Pallas kernels, whiten(): pl.pallas_call(functools.partial(whiten_kernel, size, own_count, src_coun...  81.6 us
    pallas_call x1, Pallas kernels, cross(): pl.pallas_call(cross_kernel, grid=(tiles,), in_specs=[real(count), imag(c...  46.4 us
    pallas_call x1, Pallas kernels, spatial_filter(): pl.pallas_call(functools.partial(filter_kernel, channels), grid=(samples...  9.32 us
    ppermute x1, starting transfers between devices, neighbours(): low = lax.ppermute(traces[-RIM:] * mask[-RIM:], 'fiber', up)  3.08 us
  transfers between devices with their start and end apart: 2, of which 0 were waited for; matrix products, arithmetic and copies ran while one was open for 2% of the time, Pallas kernels for 0%

profile of v2, /device:TPU:0, one launch (start us, length us, event | category | flops | bytes accessed | tf_op | source)
XLA Modules:
  0.0 149.1 jit_solution(7303009833949218931)
XLA Ops:
  0.0 0.7 fusion.2
  0.7 0.1 fusion.1
  0.8 1.6 %slice_multiply_fusion = (bf16[8,50176]{1,0:T(8,128)(2,1)S(1)}, bf16[8,50176]{1,0:T(8,128)(2,1)S(1)}) fusion(bf16[48,50176]{1,0:T(8,128)(2,1)} %own_ref.1, bf16[8]{0:T(256)(128)(2,1)S(1)} %get-tuple-element.17, bf16[8]{0:T(256)(128)(2,1)S(1)} %get-tuple-element.18), kind=kLoop, calls=%fused_computation | loop fusion | flops 802816 | bytes 3211296 | tf_op jit(solution)/shard_map/mul | solution.py:394
  2.4 1.3 collective-permute-start.1
  3.7 3.1 %collective-permute-start = (bf16[8,50176]{1,0:T(8,128)(2,1)S(1)}, bf16[8,50176]{1,0:T(8,128)(2,1)S(1)}, u32[]{:S(2)}, u32[]{:S(2)}) collective-permute-start(bf16[8,50176]{1,0:T(8,128)(2,1)S(1)} %get-tuple-element.14), channel_id=1, source_target_pairs={{0,1},{1,2},{2,3},{3,4},{4,5},{5,6},{6,7},{7,8},{8,9},{9,10},{10,1... | collective-permute-start | bytes 2408456 | tf_op jit(solution)/shard_map/ppermute | solution.py:393
  6.8 0.7 broadcast_compare_fusion
  7.4 0.7 broadcast_select_fusion
  8.2 0.1 eq.27
  8.3 0.1 iota_compare_fusion
  8.3 0.8 fusion
  9.1 0.2 select_reduce_fusion
  9.3 0.6 pad_maximum_fusion.weight_ref
  9.9 0.0 collective-permute-done.1.high_ref
  9.9 0.0 copy-start
  10.0 0.0 collective-permute-done.low_ref
  10.0 0.9 copy-done
  10.9 0.0 copy-start.1
  10.9 0.9 copy-done.1
  11.8 9.3 %spatial_filter.1 = (bf16[48,50176]{1,0:T(8,128)(2,1)}, bf16[16,50176]{1,0:T(8,128)(2,1)}) custom-call(bf16[64,64]{1,0:T(8,128)(2,1)} %pad_maximum_fusion.weight_ref, bf16[48,50176]{1,0:T(8,128)(2,1)} %own_ref.1, bf16[8,50176]{1,0:T(8,128)(2,1)} %copy-done.1, bf16[8,50176]{1,0:T(8,128)(2,1)} %copy-done), custom_call_target="tpu_custom_call" | custom-call | tf_op jit(solution)/shard_map/spatial_filter/pallas_call | solution.py:61
  21.1 81.6 %whiten.1 = (bf16[48,48,2048]{2,1,0:T(8,128)(2,1)}, bf16[48,16,2048]{2,1,0:T(8,128)(2,1)}) custom-call(bf16[48,50176]{1,0:T(8,128)(2,1)} %get-tuple-element.9.x_ref, bf16[16,50176]{1,0:T(8,128)(2,1)} %get-tuple-element.10.mine_ref, bf16[2048,2048]{1,0:T(8,128)(2,1)} %constant.19.clone.table_ref, bf16[1024,1024]{1,0:T(8,128)(2,1)} %constant.20.clone.band_ref, ...), custom_call_target="tpu_custom_call" | custom-call | flops 25769803776 | bytes 33554432 | tf_op jit(solution)/shard_map/whiten/pallas_call | solution.py:267
  102.7 46.4 %cross.1 = f32[16,48,2048]{2,1,0:T(8,128)} custom-call(bf16[48,16,2048]{2,1,0:T(8,128)(2,1)} %get-tuple-element.11.sr_ref.si_ref, bf16[48,16,2048]{2,1,0:T(8,128)(2,1)} %get-tuple-element.11.sr_ref.si_ref, bf16[48,48,2048]{2,1,0:T(8,128)(2,1)} %get-tuple-element.12.wr_ref.wi_ref, bf16[48,48,2048]{2,1,0:T(8,128)(2,1)} %get-tuple-element.12.wr_ref.wi_ref), custom_call_target="tpu_custom_call" | custom-call | tf_op jit(solution)/shard_map/cross/pallas_call | solution.py:374
  (1 shorter events, 0.0 us)
Async XLA Ops:
  2.4 7.6 %collective-permute-start.1 = (bf16[8,50176]{1,0:T(8,128)(2,1)S(1)}, bf16[8,50176]{1,0:T(8,128)(2,1)S(1)}, u32[]{:S(2)}, u32[]{:S(2)}) collective-permute-start(bf16[8,50176]{1,0:T(8,128)(2,1)S(1)} %get-tuple-element.13), channel_id=1, source_target_pairs={{1,0},{2,1},{3,2},{4,3},{5,4},{6,5},{7,6},{8,7},{9,8},{10,9},{11,1... | collective-permute-start | bytes 2408456 | tf_op jit(solution)/shard_map/ppermute | solution.py:394
  3.7 6.3 %collective-permute-start = (bf16[8,50176]{1,0:T(8,128)(2,1)S(1)}, bf16[8,50176]{1,0:T(8,128)(2,1)S(1)}, u32[]{:S(2)}, u32[]{:S(2)}) collective-permute-start(bf16[8,50176]{1,0:T(8,128)(2,1)S(1)} %get-tuple-element.14), channel_id=1, source_target_pairs={{0,1},{1,2},{2,3},{3,4},{4,5},{5,6},{6,7},{7,8},{8,9},{9,10},{10,1... | collective-permute-start | bytes 2408456 | tf_op jit(solution)/shard_map/ppermute | solution.py:393
  9.9 0.9 copy-start
  10.9 0.9 copy-start.1

commit v3 on v2

--- a/solution.py
+++ b/solution.py
@@ -121,10 +121,11 @@
     return [1 << i for i in range(size.bit_length() - 1)]
 
 
-def share_actions(size, x_ref, arrived, held, landed, result, send_sem, recv_sem):
+def share_actions(
+    size, stages, base, samples, greet,
+    x_ref, arrived, held, landed, result, send_sem, recv_sem,
+):
     me = lax.axis_index("fiber")
-    stages = share_stages(size)
-    samples = x_ref.shape[1]
     length = held.shape[2]
     sides = [lax.rem(me // bit, 2) for bit in stages]
     partners = [me + bit - 2 * bit * side for bit, side in zip(stages, sides)]
@@ -174,21 +175,22 @@
         count *= 2
 
     def enter():
-        barrier = pltpu.get_barrier_semaphore()
-        for partner in partners:
-            pl.semaphore_signal(
-                barrier,
-                inc=1,
-                device_id={"fiber": partner},
-                device_id_type=pl.DeviceIdType.MESH,
-            )
+        if greet:
+            barrier = pltpu.get_barrier_semaphore()
+            for partner in partners:
+                pl.semaphore_signal(
+                    barrier,
+                    inc=1,
+                    device_id={"fiber": partner},
+                    device_id_type=pl.DeviceIdType.MESH,
+                )
+            pl.semaphore_wait(barrier, len(stages))
         for j in range(size):
             stop = min(samples, (j + 1) * length)
             if stop < (j + 1) * length:
                 held[j] = jnp.zeros(held.shape[1:], held.dtype)
             if stop > j * length:
-                held[j, :, : stop - j * length] = x_ref[:, j * length : stop]
-        pl.semaphore_wait(barrier, len(stages))
+                held[j, :, : stop - j * length] = x_ref[:, base + j * length : base + stop]
         copies[0].start()
 
     def middle(phase):
@@ -207,7 +209,7 @@
         for j in range(size):
             stop = min(samples, (j + 1) * length)
             if stop > j * length:
-                arrived[:, j * length : stop] = result[j, :, : stop - j * length]
+                arrived[:, base + j * length : base + stop] = result[j, :, : stop - j * length]
 
     return [enter] + [middle(phase) for phase in range(1, len(copies))] + [leave]
 
@@ -216,13 +218,24 @@
     size, own_count, src_count, own_steps,
     x_ref, mine_ref, table_ref, band_ref, recip_ref,
     own_ref, src_ref,
-    spec_ref, pow_ref, arrived, held, landed, result, send_sem, recv_sem,
+    spec_ref, pow_ref, arrived, *ways,
 ):
     step = pl.program_id(0)
     tables = (table_ref, band_ref, recip_ref)
-    actions = share_actions(
-        size, mine_ref, arrived, held, landed, result, send_sem, recv_sem
-    )
+    half = mine_ref.shape[1] // 2
+    near = share_stages(size)
+    far = near[:1] + near[2:] + near[1:2]
+    one = share_actions(size, near, 0, half, True, mine_ref, arrived, *ways[:5])
+    two = share_actions(size, far, half, half, False, mine_ref, arrived, *ways[5:])
+
+    def both(first, second):
+        def run():
+            first()
+            second()
+
+        return run
+
+    actions = [both(first, second) for first, second in zip(one, two)]
     slots = 2 * own_steps
     moves = len(actions) - 1
     when = [q * slots // moves for q in range(moves)]
@@ -255,7 +268,7 @@
     sources = mine.shape[0]
     frames = samples // HOP - 1
     size = lax.axis_size("fiber")
-    length = -(-samples // (size * LANES)) * LANES
+    length = -(-samples // (2 * size * LANES)) * LANES
     phases = 2 * len(share_stages(size))
     own_steps, src_steps = frames // own_count, frames // src_count
     band, recip = band_matrix()
@@ -263,6 +276,7 @@
         shape, lambda i: (0,) * len(shape), pipeline_mode=pl.Buffered(1)
     )
     blocks = pltpu.VMEM((size, sources, length), jnp.bfloat16)
+    way = [blocks] * 3 + [pltpu.SemaphoreType.DMA((phases,))] * 2
     depth = max(own_count * rows, src_count * sources)
     return pl.pallas_call(
         functools.partial(whiten_kernel, size, own_count, src_count, own_steps),
@@ -292,11 +306,8 @@
             pltpu.VMEM((depth, FRAME), jnp.float32),
             pltpu.VMEM((depth, BINS), jnp.bfloat16),
             pltpu.VMEM((sources, samples), jnp.bfloat16),
-            blocks,
-            blocks,
-            blocks,
-            pltpu.SemaphoreType.DMA((phases,)),
-            pltpu.SemaphoreType.DMA((phases,)),
+            *way,
+            *way,
         ],
         compiler_params=pltpu.CompilerParams(
             collective_id=0, has_side_effects=True, vmem_limit_bytes=VMEM
@@ -310,18 +321,15 @@
     )(filtered, mine, dft_table(), band, recip)
 
 
-def cross_kernel(sr_ref, si_ref, wr_ref, wi_ref, out_ref, c_ref, d_ref, e_ref, a_ref, p_ref, m_ref):
+def cross_kernel(sr_ref, si_ref, wr_ref, wi_ref, out_ref, c_ref, d_ref, a_ref, p_ref, m_ref):
     frames, sources, _ = sr_ref.shape
     channels = wr_ref.shape[1]
     at = pl.multiple_of(pl.program_id(0) * LANES, LANES)
 
     @pl.loop(0, frames)
     def _(f):
-        c = wr_ref[f].astype(jnp.float32)
-        d = wi_ref[f].astype(jnp.float32)
-        c_ref[f] = c
-        d_ref[f] = d
-        e_ref[f] = c + d
+        c_ref[f] = wr_ref[f].astype(jnp.float32)
+        d_ref[f] = wi_ref[f].astype(jnp.float32)
         a = sr_ref[f].astype(jnp.float32) * (1.0 / frames)
         b = si_ref[f].astype(jnp.float32) * (1.0 / frames)
         a_ref[f] = a
@@ -329,39 +337,38 @@
         m_ref[f] = b - a
 
     pieces = channels // 8
-    together = 2
+    group = 3 if pieces % 3 == 0 else 1
+    together = 4
     for s in range(0, sources, together):
-
-        def step(f, sums):
-            sums = list(sums)
-            taps = []
-            for t in range(together):
-                row = pl.ds(s + t, 1)
-                taps.append(
-                    tuple(
+        for start in range(0, pieces, group):
+
+            def step(f, sums):
+                sums = list(sums)
+                parts = []
+                for v in range(group):
+                    part = slice(8 * (start + v), 8 * (start + v) + 8)
+                    c, d = c_ref[f, part, :], d_ref[f, part, :]
+                    parts.append((c + d, c, d))
+                for t in range(together):
+                    row = pl.ds(s + t, 1)
+                    taps = [
                         jnp.broadcast_to(ref[f, row, :], (8, LANES))
                         for ref in (a_ref, p_ref, m_ref)
-                    )
-                )
-            for v in range(pieces):
-                part = slice(8 * v, 8 * v + 8)
-                c, d, e = c_ref[f, part, :], d_ref[f, part, :], e_ref[f, part, :]
-                for t in range(together):
-                    a, p, m = taps[t]
-                    base = 3 * (t * pieces + v)
-                    sums[base] = sums[base] + a * e
-                    sums[base + 1] = sums[base + 1] + p * c
-                    sums[base + 2] = sums[base + 2] + m * d
-            return tuple(sums)
-
-        zero = jnp.zeros((8, LANES), jnp.float32)
-        sums = lax.fori_loop(0, frames, step, (zero,) * (3 * together * pieces), unroll=4)
-        for t in range(together):
-            for v in range(pieces):
-                base = 3 * (t * pieces + v)
-                part = slice(8 * v, 8 * v + 8)
-                out_ref[s + t, part, pl.ds(at, LANES)] = sums[base] + sums[base + 2]
-                out_ref[s + t, part, pl.ds(BINS + at, LANES)] = sums[base] - sums[base + 1]
+                    ]
+                    for v in range(group):
+                        for u in range(3):
+                            base = 3 * (t * group + v) + u
+                            sums[base] = sums[base] + taps[u] * parts[v][u]
+                return tuple(sums)
+
+            zero = jnp.zeros((8, LANES), jnp.float32)
+            sums = lax.fori_loop(0, frames, step, (zero,) * (3 * together * group), unroll=4)
+            for t in range(together):
+                for v in range(group):
+                    one, two, three = sums[3 * (t * group + v) : 3 * (t * group + v) + 3]
+                    part = slice(8 * (start + v), 8 * (start + v) + 8)
+                    out_ref[s + t, part, pl.ds(at, LANES)] = one + three
+                    out_ref[s + t, part, pl.ds(BINS + at, LANES)] = one - two
 
 
 def cross(sources, whitened):
@@ -379,7 +386,7 @@
             (count, channels, FRAME), lambda j: (0, 0, 0), pipeline_mode=pl.Buffered(1)
         ),
         out_shape=jax.ShapeDtypeStruct((count, channels, FRAME), jnp.float32),
-        scratch_shapes=[tile(channels)] * 3 + [tile(count)] * 3,
+        scratch_shapes=[tile(channels)] * 2 + [tile(count)] * 3,
         compiler_params=pltpu.CompilerParams(vmem_limit_bytes=VMEM),
         name="cross",
     )(sources, sources, whitened, whitened)

time: 150 us -> 144 us (0.960)
  Pallas kernels: 137 us -> 131 us
    pallas_call x1, Pallas kernels: 81.6 us -> 75.2 us  [whiten(): pl.pallas_call(functools.partial(whiten_kernel, size, own_count, src_coun...]
where the time goes in v3:
time: 144 us; the launch traced here: 143 us
  Pallas kernels  131 us (91%)
  other arithmetic  5.38 us (4%)
  starting transfers between devices  4.37 us (3%)
  local copies, waits for them, and re-layouts  1.97 us (1%)
    pallas_call x1, Pallas kernels, whiten(): pl.pallas_call(functools.partial(whiten_kernel, size, own_count, src_coun...  75.2 us
    pallas_call x1, Pallas kernels, cross(): pl.pallas_call(cross_kernel, grid=(tiles,), in_specs=[real(count), imag(c...  46.8 us
    pallas_call x1, Pallas kernels, spatial_filter(): pl.pallas_call(functools.partial(filter_kernel, channels), grid=(samples...  9.32 us
    ppermute x1, starting transfers between devices, neighbours(): low = lax.ppermute(traces[-RIM:] * mask[-RIM:], 'fiber', up)  3.08 us
  transfers between devices with their start and end apart: 2, of which 0 were waited for; matrix products, arithmetic and copies ran while one was open for 2% of the time, Pallas kernels for 0%

profile of v3, /device:TPU:0, one launch (start us, length us, event | category | flops | bytes accessed | tf_op | source)
XLA Modules:
  0.0 143.2 jit_solution(14347399915112846750)
XLA Ops:
  0.0 0.7 fusion.2
  0.7 0.1 fusion.1
  0.8 1.6 %slice_multiply_fusion = (bf16[8,50176]{1,0:T(8,128)(2,1)S(1)}, bf16[8,50176]{1,0:T(8,128)(2,1)S(1)}) fusion(bf16[48,50176]{1,0:T(8,128)(2,1)} %own_ref.1, bf16[8]{0:T(256)(128)(2,1)S(1)} %get-tuple-element.17, bf16[8]{0:T(256)(128)(2,1)S(1)} %get-tuple-element.18), kind=kLoop, calls=%fused_computation | loop fusion | flops 802816 | bytes 3211296 | tf_op jit(solution)/shard_map/mul | solution.py:401
  2.4 1.3 collective-permute-start.1
  3.7 3.1 %collective-permute-start = (bf16[8,50176]{1,0:T(8,128)(2,1)S(1)}, bf16[8,50176]{1,0:T(8,128)(2,1)S(1)}, u32[]{:S(2)}, u32[]{:S(2)}) collective-permute-start(bf16[8,50176]{1,0:T(8,128)(2,1)S(1)} %get-tuple-element.14), channel_id=1, source_target_pairs={{0,1},{1,2},{2,3},{3,4},{4,5},{5,6},{6,7},{7,8},{8,9},{9,10},{10,1... | collective-permute-start | bytes 2408456 | tf_op jit(solution)/shard_map/ppermute | solution.py:400
  6.8 0.7 broadcast_compare_fusion
  7.4 0.7 broadcast_select_fusion
  8.2 0.1 eq.27
  8.3 0.1 iota_compare_fusion
  8.3 0.8 fusion
  9.1 0.2 select_reduce_fusion
  9.3 0.6 pad_maximum_fusion.weight_ref
  9.9 0.0 collective-permute-done.1.high_ref
  9.9 0.0 copy-start
  10.0 0.0 collective-permute-done.low_ref
  10.0 0.9 copy-done
  10.9 0.0 copy-start.1
  10.9 0.9 copy-done.1
  11.8 9.3 %spatial_filter.1 = (bf16[48,50176]{1,0:T(8,128)(2,1)}, bf16[16,50176]{1,0:T(8,128)(2,1)}) custom-call(bf16[64,64]{1,0:T(8,128)(2,1)} %pad_maximum_fusion.weight_ref, bf16[48,50176]{1,0:T(8,128)(2,1)} %own_ref.1, bf16[8,50176]{1,0:T(8,128)(2,1)} %copy-done.1, bf16[8,50176]{1,0:T(8,128)(2,1)} %copy-done), custom_call_target="tpu_custom_call" | custom-call | tf_op jit(solution)/shard_map/spatial_filter/pallas_call | solution.py:61
  21.1 75.2 %whiten.1 = (bf16[48,48,2048]{2,1,0:T(8,128)(2,1)}, bf16[48,16,2048]{2,1,0:T(8,128)(2,1)}) custom-call(bf16[48,50176]{1,0:T(8,128)(2,1)} %get-tuple-element.9.x_ref, bf16[16,50176]{1,0:T(8,128)(2,1)} %get-tuple-element.10.mine_ref, bf16[2048,2048]{1,0:T(8,128)(2,1)} %constant.19.clone.table_ref, bf16[1024,1024]{1,0:T(8,128)(2,1)} %constant.20.clone.band_ref, ...), custom_call_target="tpu_custom_call" | custom-call | flops 25769803776 | bytes 33554432 | tf_op jit(solution)/shard_map/whiten/pallas_call | solution.py:281
  96.3 46.8 %cross.1 = f32[16,48,2048]{2,1,0:T(8,128)} custom-call(bf16[48,16,2048]{2,1,0:T(8,128)(2,1)} %get-tuple-element.11.sr_ref.si_ref, bf16[48,16,2048]{2,1,0:T(8,128)(2,1)} %get-tuple-element.11.sr_ref.si_ref, bf16[48,48,2048]{2,1,0:T(8,128)(2,1)} %get-tuple-element.12.wr_ref.wi_ref, bf16[48,48,2048]{2,1,0:T(8,128)(2,1)} %get-tuple-element.12.wr_ref.wi_ref), custom_call_target="tpu_custom_call" | custom-call | tf_op jit(solution)/shard_map/cross/pallas_call | solution.py:381
  (1 shorter events, 0.0 us)
Async XLA Ops:
  2.4 7.6 %collective-permute-start.1 = (bf16[8,50176]{1,0:T(8,128)(2,1)S(1)}, bf16[8,50176]{1,0:T(8,128)(2,1)S(1)}, u32[]{:S(2)}, u32[]{:S(2)}) collective-permute-start(bf16[8,50176]{1,0:T(8,128)(2,1)S(1)} %get-tuple-element.13), channel_id=1, source_target_pairs={{1,0},{2,1},{3,2},{4,3},{5,4},{6,5},{7,6},{8,7},{9,8},{10,9},{11,1... | collective-permute-start | bytes 2408456 | tf_op jit(solution)/shard_map/ppermute | solution.py:401
  3.7 6.3 %collective-permute-start = (bf16[8,50176]{1,0:T(8,128)(2,1)S(1)}, bf16[8,50176]{1,0:T(8,128)(2,1)S(1)}, u32[]{:S(2)}, u32[]{:S(2)}) collective-permute-start(bf16[8,50176]{1,0:T(8,128)(2,1)S(1)} %get-tuple-element.14), channel_id=1, source_target_pairs={{0,1},{1,2},{2,3},{3,4},{4,5},{5,6},{6,7},{7,8},{8,9},{9,10},{10,1... | collective-permute-start | bytes 2408456 | tf_op jit(solution)/shard_map/ppermute | solution.py:400
  9.9 0.9 copy-start
  10.9 0.9 copy-start.1
